TPU v7x, 128 devices: a whole 4x4x4 slice. The times are simulated.
128 devices in a mesh: tm: 32 (over z, y, x_lo), slab: 4 (over x_hi, core).
Axes of the slice: x: 4 (x_hi: 2, x_lo: 2; x = x_hi * 2 + x_lo), y: 4, z: 4, core: 2. Of those that a mesh axis runs over, the one named last changes fastest.
Arguments:
- kspace: bfloat16 [2, 64, 4, 96, 9984], P(None, 'tm', None, 'slab'), may hold values from -40 to 40, as said below
- sens: float32 [2, 4, 8, 104, 96], P(None, None, None, 'slab'), may hold values from -3 to 3
Outputs:
- projected: float32 [64, 2, 8, 104, 96], P('tm', None, None, 'slab')
Inputs may be any that keep to these rules, and one draw needn't show every extreme that they name: `kspace`: k-space values of order one with frames of different scale.
All inputs are finite; a program needn't handle non-finite values.
Results may differ from a plain program's by a relative error of at most 0.0036.
Values may be sent and summed in bfloat16 or wider, within the bound.
A program may use at most 128 MiB of HBM per device.

v0:
```python
import jax
import jax.numpy as jnp
from jax import lax
from jax.sharding import PartitionSpec as P

NX = 96
NY = 104
NZ = 96
RANK = 32
ITERS = 4
XW = 8


def inverse_table(length, count, offset):
    outputs = jnp.arange(count, dtype=jnp.int32) + offset
    inputs = jnp.arange(length, dtype=jnp.int32)
    phase = outputs[:, None] * inputs[None, :] % length
    angle = phase.astype(jnp.float32) * (2.0 * jnp.pi / length)
    norm_factor = 1.0 / jnp.sqrt(jnp.float32(length))
    return (jnp.cos(angle) * norm_factor, jnp.sin(angle) * norm_factor)


def contract(pattern, matrix_table, operand):
    return jnp.einsum(pattern, matrix_table, operand, precision=lax.Precision.HIGHEST)


def matmul(left, right):
    return jnp.dot(left, right, precision=lax.Precision.HIGHEST)


def orthonormal(rows, gram):
    factor = jnp.linalg.cholesky(matmul(matmul(rows, gram), rows.T))
    return lax.linalg.triangular_solve(factor, rows, left_side=True, lower=True)


def local(kspace, sens):
    frames_dev = kspace.shape[1]
    coil_count = kspace.shape[2]
    depth_dev = kspace.shape[3]
    spectrum = kspace.astype(jnp.float32).reshape(2, frames_dev, coil_count, depth_dev, NX, NY)
    across_cos, across_sin = inverse_table(NX, XW, (NX - XW) // 2)
    down_cos, down_sin = inverse_table(NY, NY, 0)
    depth_cos, depth_sin = inverse_table(NZ, NZ, 0)
    across_real = contract("jx,fczxy->fczjy", across_cos, spectrum[0]) - contract(
        "jx,fczxy->fczjy", across_sin, spectrum[1]
    )
    across_other = contract("jx,fczxy->fczjy", across_cos, spectrum[1]) + contract(
        "jx,fczxy->fczjy", across_sin, spectrum[0]
    )
    down_real = contract("my,fczjy->fczjm", down_cos, across_real) - contract(
        "my,fczjy->fczjm", down_sin, across_other
    )
    down_other = contract("my,fczjy->fczjm", down_cos, across_other) + contract(
        "my,fczjy->fczjm", down_sin, across_real
    )
    planes = jnp.stack([down_real, down_other]).astype(jnp.bfloat16)
    arrived = lax.all_to_all(planes, "slab", split_axis=5, concat_axis=3, tiled=True).astype(
        jnp.float32
    )
    depth_real = contract("wz,fczxy->fcxyw", depth_cos, arrived[0]) - contract(
        "wz,fczxy->fcxyw", depth_sin, arrived[1]
    )
    depth_other = contract("wz,fczxy->fcxyw", depth_cos, arrived[1]) + contract(
        "wz,fczxy->fcxyw", depth_sin, arrived[0]
    )
    sens_real = sens[0][None]
    sens_other = sens[1][None]
    combined_real = jnp.sum(sens_real * depth_real + sens_other * depth_other, axis=1)
    combined_other = jnp.sum(sens_real * depth_other - sens_other * depth_real, axis=1)
    matrix = jnp.stack([combined_real, combined_other], axis=1).reshape(frames_dev, -1)
    rows = lax.all_to_all(matrix, "tm", split_axis=1, concat_axis=0, tiled=True)
    gram = lax.psum(matmul(rows, rows.T), ("tm", "slab"))
    eye = jnp.eye(RANK, dtype=jnp.float32)
    current = jnp.concatenate([eye, eye], axis=1)
    for sweep_index in range(ITERS):
        current = matmul(orthonormal(current, gram), gram)
    coeff = orthonormal(current, gram)
    mixing = matmul(matmul(coeff, gram).T, coeff)
    projected = matmul(mixing, rows)
    projected = lax.all_to_all(projected, "tm", split_axis=0, concat_axis=1, tiled=True)
    return projected.reshape(frames_dev, 2, XW, -1, NZ)


def solution(mesh):
    in_specs = (P(None, "tm", None, "slab", None), P(None, None, None, "slab", None))
    out_specs = P("tm", None, None, "slab", None)
    return jax.shard_map(local, mesh=mesh, in_specs=in_specs, out_specs=out_specs, check_vma=False)
```

profile of v0, /device:TPU:0, one launch (start us, length us, event | category | flops | bytes accessed | tf_op | source)
XLA Modules:
  0.0 234.5 jit_solution(5598859404871233806)
XLA Ops:
  0.0 5.4 %fusion.180 = (bf16[1,2,4,24,9984]{4,3,2,1,0:T(8,128)(2,1)}, bf16[1,2,4,24,9984]{4,3,2,1,0:T(8,128)(2,1)}) fusion(bf16[2,2,4,24,9984]{4,3,2,1,0:T(8,128)(2,1)} %param.5), kind=kLoop, calls=%fused_computation.213 | loop fusion | bytes 15335424 | tf_op jit(solution)/shard_map/slice | solution.py:44
  5.4 13.7 %squeeze.16 = bf16[2,4,24,96,104]{4,3,2,1,0:T(8,128)(2,1)} reshape(bf16[1,2,4,24,9984]{4,3,2,1,0:T(8,128)(2,1)} %get-tuple-element.9) | data formatting | bytes 7667712 | tf_op jit(solution)/shard_map/squeeze | solution.py:44
  19.2 13.8 %squeeze.17 = bf16[2,4,24,96,104]{4,3,2,1,0:T(8,128)(2,1)} reshape(bf16[1,2,4,24,9984]{4,3,2,1,0:T(8,128)(2,1)} %get-tuple-element.10) | data formatting | bytes 7667712 | tf_op jit(solution)/shard_map/squeeze | solution.py:45
  33.0 4.3 %fusion.105 = f32[8,2,4,24,104]{4,0,3,2,1:T(8,128)S(1)} fusion(bf16[2,4,24,96,104]{4,3,2,1,0:T(8,128)(2,1)} %squeeze.16, s32[8]{0:T(128)S(1)} %iota_add_fusion), kind=kOutput, calls=%fused_computation.133 | convolution fusion | flops 184032768 | bytes 4472864 | tf_op jit(solution)/shard_map/jx,fczxy->fczjy/dot_general | solution.py:24
  48.6 5.8 %copy.42 = bf16[2,2,4,24,8,104]{3,4,2,1,0,5:T(8,128)(2,1)S(1)} copy(bf16[2,2,4,24,8,104]{5,3,4,2,1,0:T(8,128)(2,1)} %pad_maximum_fusion) | data formatting | bytes 1277952 | tf_op jit(solution)/shard_map/stack | solution.py:56
  54.4 5.0 %reshape.64 = bf16[4,2,39936]{2,1,0:T(2,128)(2,1)} reshape(bf16[104,2,2,4,8,24]{5,4,3,2,1,0:T(8,128)(2,1)S(1)} %bitcast.164) | data formatting | bytes 1277952
  59.4 4.4 %all-to-all-start = ((bf16[4,2,39936]{2,1,0:T(2,128)(2,1)}), bf16[4,2,39936]{2,1,0:T(2,128)(2,1)}, u32[]{:S(2)}, u32[]{:S(2)}) async-start(bf16[4,2,39936]{2,1,0:T(2,128)(2,1)} %reshape.64), calls=%async_computation | async-start | bytes 1277952 | tf_op jit(solution)/shard_map/all_to_all | solution.py:57
  66.8 8.7 %all-to-all-done = bf16[4,2,39936]{2,1,0:T(2,128)(2,1)} async-done(((bf16[4,2,39936]{2,1,0:T(2,128)(2,1)}), bf16[4,2,39936]{2,1,0:T(2,128)(2,1)}, u32[]{:S(2)}, u32[]{:S(2)}) %all-to-all-start) | async-done | bytes 639008 | tf_op jit(solution)/shard_map/all_to_all | solution.py:57
  75.5 5.6 %reshape.65 = bf16[104,2,2,4,8,24]{5,4,3,2,1,0:T(8,128)(2,1)S(1)} reshape(bf16[4,2,39936]{2,1,0:T(2,128)(2,1)} %all-to-all-done) | data formatting | bytes 1277952
  81.1 4.4 %copy.86 = bf16[2,2,4,24,8,4,26]{3,5,4,6,2,1,0:T(4,128)(2,1)S(1)} copy(bf16[2,2,4,24,8,4,26]{3,4,2,1,0,6,5:T(8,128)(2,1)S(1)} %bitcast.165) | data formatting | bytes 1277952 | tf_op jit(solution)/shard_map/all_to_all | solution.py:57
  88.3 2.9 %fusion.16 = f32[2,4,8,26,96]{4,3,2,1,0:T(8,128)} fusion(bf16[2,4,96,8,26]{2,3,4,1,0:T(8,128)(2,1)} %squeeze.18), kind=kOutput, calls=%fused_computation.27 | convolution fusion | flops 184117248 | bytes 958464 | tf_op jit(solution)/shard_map/wz,fczxy->fcxyw/dot_general | solution.py:24
  98.3 9.4 %all-to-all-start.1 = ((f32[2,32,1248]{2,0,1:T(2,128)}), f32[2,32,1248]{2,0,1:T(2,128)S(1)}, u32[]{:S(2)}, u32[]{:S(2)}) async-start(f32[2,32,1248]{2,0,1:T(2,128)} %copy.49), calls=%async_computation.1 | async-start | bytes 655360 | tf_op jit(solution)/shard_map/all_to_all | solution.py:71
  107.7 9.6 %all-to-all-done.1 = f32[2,32,1248]{2,0,1:T(2,128)S(1)} async-done(((f32[2,32,1248]{2,0,1:T(2,128)}), f32[2,32,1248]{2,0,1:T(2,128)S(1)}, u32[]{:S(2)}, u32[]{:S(2)}) %all-to-all-start.1) | async-done | bytes 319520 | tf_op jit(solution)/shard_map/all_to_all | solution.py:71
  118.2 62.4 %psum.7 = f32[64,64]{1,0:T(8,128)S(1)} all-reduce(f32[64,64]{1,0:T(8,128)S(1)} %fusion.182), channel_id=1, replica_groups=mesh['tm'=32,'slab'=4] {'tm','slab'}, use_global_device_ids=true, to_apply=%region_2.3 | all-reduce | flops 4096 | bytes 32768 | tf_op jit(solution)/shard_map/psum | solution.py:72
  181.1 2.9 %cholesky.89 = f32[32,32]{1,0:T(8,128)S(1)} custom-call(f32[32,32]{1,0:T(8,128)S(1)} %fusion.89), custom_call_target="Cholesky" | custom-call | tf_op jit(solution)/shard_map/jit(cholesky)/cholesky | solution.py:32
  185.4 2.4 %custom-call.9 = f32[1,32,32]{1,2,0:T(8,128)S(1)} custom-call(f32[1,32,32]{2,1,0:T(8,128)S(1)} %fusion.70), custom_call_target="InvertDiagBlocksLowerTriangular" | custom-call | tf_op jit(solution)/shard_map/triangular_solve/custom-call.0 | solution.py:33
  188.6 2.9 %cholesky.100 = f32[32,32]{1,0:T(8,128)S(1)} custom-call(f32[32,32]{1,0:T(8,128)S(1)} %fusion.86), custom_call_target="Cholesky" | custom-call | tf_op jit(solution)/shard_map/jit(cholesky)/cholesky | solution.py:32
  192.9 2.4 %custom-call.10 = f32[1,32,32]{1,2,0:T(8,128)S(1)} custom-call(f32[1,32,32]{2,1,0:T(8,128)S(1)} %fusion.71), custom_call_target="InvertDiagBlocksLowerTriangular" | custom-call | tf_op jit(solution)/shard_map/triangular_solve/custom-call.0 | solution.py:33
  196.1 2.9 %cholesky.111 = f32[32,32]{1,0:T(8,128)S(1)} custom-call(f32[32,32]{1,0:T(8,128)S(1)} %fusion.83), custom_call_target="Cholesky" | custom-call | tf_op jit(solution)/shard_map/jit(cholesky)/cholesky | solution.py:32
  200.4 2.4 %custom-call.11 = f32[1,32,32]{1,2,0:T(8,128)S(1)} custom-call(f32[1,32,32]{2,1,0:T(8,128)S(1)} %fusion.72), custom_call_target="InvertDiagBlocksLowerTriangular" | custom-call | tf_op jit(solution)/shard_map/triangular_solve/custom-call.0 | solution.py:33
  203.6 2.9 %cholesky.122 = f32[32,32]{1,0:T(8,128)S(1)} custom-call(f32[32,32]{1,0:T(8,128)S(1)} %fusion.80), custom_call_target="Cholesky" | custom-call | tf_op jit(solution)/shard_map/jit(cholesky)/cholesky | solution.py:32
  207.8 2.4 %custom-call.12 = f32[1,32,32]{1,2,0:T(8,128)S(1)} custom-call(f32[1,32,32]{2,1,0:T(8,128)S(1)} %fusion.73), custom_call_target="InvertDiagBlocksLowerTriangular" | custom-call | tf_op jit(solution)/shard_map/triangular_solve/custom-call.0 | solution.py:33
  211.1 2.9 %cholesky.133 = f32[32,32]{1,0:T(8,128)S(1)} custom-call(f32[32,32]{1,0:T(8,128)S(1)} %fusion.77), custom_call_target="Cholesky" | custom-call | tf_op jit(solution)/shard_map/jit(cholesky)/cholesky | solution.py:32
  219.1 14.0 %all_to_all.47 = f32[32,2,1248]{2,1,0:T(2,128)S(1)} all-to-all(f32[32,2,1248]{2,1,0:T(2,128)S(1)} %copy.56), channel_id=1, replica_groups=mesh['tm'=32,'slab'=4] {'tm'}, dimensions={0} | all-to-all | bytes 638976 | tf_op jit(solution)/shard_map/all_to_all | solution.py:80
  (88 shorter events, 40.2 us)
Async XLA Ops:
  33.0 4.3 %copy-start = (bf16[2,4,24,96,104]{4,3,2,1,0:T(8,128)(2,1)S(1)}, bf16[2,4,24,96,104]{4,3,2,1,0:T(8,128)(2,1)}, u32[]{:S(2)}) copy-start(bf16[2,4,24,96,104]{4,3,2,1,0:T(8,128)(2,1)} %squeeze.17) | copy-start | bytes 11501572
  37.3 5.1 %slice-start = ((s8[4718592]{0:T(1024)(128)(4,1)}), s8[4194304]{0:T(1024)(128)(4,1)S(1)}, s32[]{:S(2)}) async-start(s8[4718592]{0:T(1024)(128)(4,1)} %bitcast.161), calls=%async_computation.3 | async-start | bytes 8388608
  39.4 3.1 %slice-start.1 = ((s8[4718592]{0:T(1024)(128)(4,1)}), s8[524288]{0:T(1024)(128)(4,1)S(1)}, s32[]{:S(2)}) async-start(s8[4718592]{0:T(1024)(128)(4,1)} %bitcast.161), calls=%async_computation.4 | async-start | bytes 1048576
  59.4 16.1 %all-to-all-start = ((bf16[4,2,39936]{2,1,0:T(2,128)(2,1)}), bf16[4,2,39936]{2,1,0:T(2,128)(2,1)}, u32[]{:S(2)}, u32[]{:S(2)}) async-start(bf16[4,2,39936]{2,1,0:T(2,128)(2,1)} %reshape.64), calls=%async_computation | async-start | bytes 1277952 | tf_op jit(solution)/shard_map/all_to_all | solution.py:57
  88.3 6.6 %copy-start.1 = (bf16[2,4,96,8,26]{2,3,4,1,0:T(8,128)(2,1)S(1)}, bf16[2,4,96,8,26]{2,3,4,1,0:T(8,128)(2,1)}, u32[]{:S(2)}) copy-start(bf16[2,4,96,8,26]{2,3,4,1,0:T(8,128)(2,1)} %squeeze.18) | copy-start | bytes 958468
  88.3 6.6 %copy-start.2 = (f32[4,8,26,96]{3,2,1,0:T(8,128)S(1)}, f32[4,8,26,96]{3,2,1,0:T(8,128)}, u32[]{:S(2)}) copy-start(f32[4,8,26,96]{3,2,1,0:T(8,128)} %copy.37) | copy-start | bytes 958468
  98.3 19.0 %all-to-all-start.1 = ((f32[2,32,1248]{2,0,1:T(2,128)}), f32[2,32,1248]{2,0,1:T(2,128)S(1)}, u32[]{:S(2)}, u32[]{:S(2)}) async-start(f32[2,32,1248]{2,0,1:T(2,128)} %copy.49), calls=%async_computation.1 | async-start | bytes 655360 | tf_op jit(solution)/shard_map/all_to_all | solution.py:71
where the time goes:
time: 235 us; the launch traced here: 234 us
  blocking collectives  76.4 us (33%)
  local copies, waits for them, and re-layouts  64.1 us (27%)
  other arithmetic  34.6 us (15%)
  matrix products  26.8 us (11%)
  waiting for transfers between devices  18.3 us (8%)
  starting transfers between devices  13.7 us (6%)
    psum x1, blocking collectives, local(): gram = lax.psum(matmul(rows, rows.T), ('tm', 'slab'))  62.4 us
    dot_general x12, matrix products, contract(): jnp.einsum(pattern, matrix_table, operand, precision=lax.Precision.HIGHEST)  22.3 us
    another operation x16, other arithmetic, orthonormal(): factor = jnp.linalg.cholesky(matmul(matmul(rows, gram), rows.T))  18 us
    another operation x10, other arithmetic, orthonormal(): return lax.linalg.triangular_solve(factor, rows, left_side=True, lower=True)  15.4 us
    all_to_all x1, blocking collectives, local(): lax.all_to_all(projected, 'tm', split_axis=0, concat_axis=1, tiled=True)  14 us
    squeeze x1, local copies, waits for them, and re-layouts, local(): spectrum[1]  13.8 us
    squeeze x1, local copies, waits for them, and re-layouts, local(): spectrum[0]  13.7 us
    unnamed x12, local copies, waits for them, and re-layouts  10.6 us
  transfers between devices with their start and end apart: 2, of which 2 were waited for; matrix products, arithmetic and copies ran while one was open for 1% of the time, Pallas kernels for 0%

commit v1 on v0

--- a/solution.py
+++ b/solution.py
@@ -77,7 +77,10 @@
     coeff = orthonormal(current, gram)
     mixing = matmul(matmul(coeff, gram).T, coeff)
     projected = matmul(mixing, rows)
-    projected = lax.all_to_all(projected, "tm", split_axis=0, concat_axis=1, tiled=True)
+    projected = jnp.concatenate(
+        lax.all_to_all(jnp.stack(jnp.split(projected, lax.axis_size("tm"), axis=0)), "tm", 0, 0),
+        axis=1,
+    )
     return projected.reshape(frames_dev, 2, XW, -1, NZ)
 
 

time: 235 us -> 235 us (level)
    unnamed x12 -> x43, local copies, waits for them, and re-layouts: 10.6 us -> 11 us
where the time goes in v1:
time: 235 us
  blocking collectives  76.5 us (33%)
  local copies, waits for them, and re-layouts  64 us (27%)
  other arithmetic  34.6 us (15%)
  matrix products  26.8 us (11%)
  waiting for transfers between devices  18.3 us (8%)
  starting transfers between devices  13.7 us (6%)
    psum x1, blocking collectives, local(): gram = lax.psum(matmul(rows, rows.T), ('tm', 'slab'))  62.4 us
    dot_general x12, matrix products, contract(): jnp.einsum(pattern, matrix_table, operand, precision=lax.Precision.HIGHEST)  22.3 us
    another operation x16, other arithmetic, orthonormal(): factor = jnp.linalg.cholesky(matmul(matmul(rows, gram), rows.T))  18 us
    another operation x10, other arithmetic, orthonormal(): return lax.linalg.triangular_solve(factor, rows, left_side=True, lower=True)  15.4 us
    all_to_all x1, blocking collectives, local(): lax.all_to_all(jnp.stack(jnp.split(projected, lax.axis_size('tm'), axis=0...  14 us
    squeeze x1, local copies, waits for them, and re-layouts, local(): spectrum[1]  13.8 us
    squeeze x1, local copies, waits for them, and re-layouts, local(): spectrum[0]  13.7 us
    unnamed x43, local copies, waits for them, and re-layouts  11 us
  transfers between devices with their start and end apart: 2, of which 2 were waited for; matrix products, arithmetic and copies ran while one was open for 1% of the time, Pallas kernels for 0%

profile of v1, /device:TPU:0, one launch (start us, length us, event | category | flops | bytes accessed | tf_op | source)
XLA Modules:
  0.0 234.5 jit_solution(14831246014550155394)
XLA Ops:
  0.0 5.4 %fusion.178 = (bf16[1,2,4,24,9984]{4,3,2,1,0:T(8,128)(2,1)}, bf16[1,2,4,24,9984]{4,3,2,1,0:T(8,128)(2,1)}) fusion(bf16[2,2,4,24,9984]{4,3,2,1,0:T(8,128)(2,1)} %param.5), kind=kLoop, calls=%fused_computation.275 | loop fusion | bytes 15335424 | tf_op jit(solution)/shard_map/slice | solution.py:44
  5.4 13.7 %squeeze.16 = bf16[2,4,24,96,104]{4,3,2,1,0:T(8,128)(2,1)} reshape(bf16[1,2,4,24,9984]{4,3,2,1,0:T(8,128)(2,1)} %get-tuple-element.9) | data formatting | bytes 7667712 | tf_op jit(solution)/shard_map/squeeze | solution.py:44
  19.2 13.8 %squeeze.17 = bf16[2,4,24,96,104]{4,3,2,1,0:T(8,128)(2,1)} reshape(bf16[1,2,4,24,9984]{4,3,2,1,0:T(8,128)(2,1)} %get-tuple-element.10) | data formatting | bytes 7667712 | tf_op jit(solution)/shard_map/squeeze | solution.py:45
  33.0 4.3 %fusion.103 = f32[8,2,4,24,104]{4,0,3,2,1:T(8,128)S(1)} fusion(bf16[2,4,24,96,104]{4,3,2,1,0:T(8,128)(2,1)} %squeeze.16, s32[8]{0:T(128)S(1)} %iota_add_fusion), kind=kOutput, calls=%fused_computation.195 | convolution fusion | flops 184032768 | bytes 4472864 | tf_op jit(solution)/shard_map/jx,fczxy->fczjy/dot_general | solution.py:24
  48.6 5.8 %copy.40 = bf16[2,2,4,24,8,104]{3,4,2,1,0,5:T(8,128)(2,1)S(1)} copy(bf16[2,2,4,24,8,104]{5,3,4,2,1,0:T(8,128)(2,1)} %pad_maximum_fusion) | data formatting | bytes 1277952 | tf_op jit(solution)/shard_map/stack | solution.py:56
  54.4 5.0 %reshape.57 = bf16[4,2,39936]{2,1,0:T(2,128)(2,1)} reshape(bf16[104,2,2,4,8,24]{5,4,3,2,1,0:T(8,128)(2,1)S(1)} %bitcast.292) | data formatting | bytes 1277952
  59.4 4.4 %all-to-all-start = ((bf16[4,2,39936]{2,1,0:T(2,128)(2,1)}), bf16[4,2,39936]{2,1,0:T(2,128)(2,1)}, u32[]{:S(2)}, u32[]{:S(2)}) async-start(bf16[4,2,39936]{2,1,0:T(2,128)(2,1)} %reshape.57), calls=%async_computation | async-start | bytes 1277952 | tf_op jit(solution)/shard_map/all_to_all | solution.py:57
  66.8 8.7 %all-to-all-done = bf16[4,2,39936]{2,1,0:T(2,128)(2,1)} async-done(((bf16[4,2,39936]{2,1,0:T(2,128)(2,1)}), bf16[4,2,39936]{2,1,0:T(2,128)(2,1)}, u32[]{:S(2)}, u32[]{:S(2)}) %all-to-all-start) | async-done | bytes 639008 | tf_op jit(solution)/shard_map/all_to_all | solution.py:57
  75.5 5.6 %reshape.58 = bf16[104,2,2,4,8,24]{5,4,3,2,1,0:T(8,128)(2,1)S(1)} reshape(bf16[4,2,39936]{2,1,0:T(2,128)(2,1)} %all-to-all-done) | data formatting | bytes 1277952
  81.1 4.4 %copy.80 = bf16[2,2,4,24,8,4,26]{3,5,4,6,2,1,0:T(4,128)(2,1)S(1)} copy(bf16[2,2,4,24,8,4,26]{3,4,2,1,0,6,5:T(8,128)(2,1)S(1)} %bitcast.293) | data formatting | bytes 1277952 | tf_op jit(solution)/shard_map/all_to_all | solution.py:57
  88.3 2.9 %fusion.16 = f32[2,4,8,26,96]{4,3,2,1,0:T(8,128)} fusion(bf16[2,4,96,8,26]{2,3,4,1,0:T(8,128)(2,1)} %squeeze.18), kind=kOutput, calls=%fused_computation.27 | convolution fusion | flops 184117248 | bytes 958464 | tf_op jit(solution)/shard_map/wz,fczxy->fcxyw/dot_general | solution.py:24
  98.3 9.4 %all-to-all-start.1 = ((f32[2,32,1248]{2,0,1:T(2,128)}), f32[2,32,1248]{2,0,1:T(2,128)S(1)}, u32[]{:S(2)}, u32[]{:S(2)}) async-start(f32[2,32,1248]{2,0,1:T(2,128)} %copy.47), calls=%async_computation.1 | async-start | bytes 655360 | tf_op jit(solution)/shard_map/all_to_all | solution.py:71
  107.7 9.6 %all-to-all-done.1 = f32[2,32,1248]{2,0,1:T(2,128)S(1)} async-done(((f32[2,32,1248]{2,0,1:T(2,128)}), f32[2,32,1248]{2,0,1:T(2,128)S(1)}, u32[]{:S(2)}, u32[]{:S(2)}) %all-to-all-start.1) | async-done | bytes 319520 | tf_op jit(solution)/shard_map/all_to_all | solution.py:71
  117.9 62.4 %psum.7 = f32[64,64]{1,0:T(8,128)S(1)} all-reduce(f32[64,64]{1,0:T(8,128)S(1)} %fusion.180), channel_id=1, replica_groups=mesh['tm'=32,'slab'=4] {'tm','slab'}, use_global_device_ids=true, to_apply=%region_2.3 | all-reduce | flops 4096 | bytes 32768 | tf_op jit(solution)/shard_map/psum | solution.py:72
  180.9 2.9 %cholesky.89 = f32[32,32]{1,0:T(8,128)S(1)} custom-call(f32[32,32]{1,0:T(8,128)S(1)} %fusion.87), custom_call_target="Cholesky" | custom-call | tf_op jit(solution)/shard_map/jit(cholesky)/cholesky | solution.py:32
  185.1 2.4 %custom-call.9 = f32[1,32,32]{1,2,0:T(8,128)S(1)} custom-call(f32[1,32,32]{2,1,0:T(8,128)S(1)} %fusion.68), custom_call_target="InvertDiagBlocksLowerTriangular" | custom-call | tf_op jit(solution)/shard_map/triangular_solve/custom-call.0 | solution.py:33
  188.4 2.9 %cholesky.100 = f32[32,32]{1,0:T(8,128)S(1)} custom-call(f32[32,32]{1,0:T(8,128)S(1)} %fusion.84), custom_call_target="Cholesky" | custom-call | tf_op jit(solution)/shard_map/jit(cholesky)/cholesky | solution.py:32
  192.6 2.4 %custom-call.10 = f32[1,32,32]{1,2,0:T(8,128)S(1)} custom-call(f32[1,32,32]{2,1,0:T(8,128)S(1)} %fusion.69), custom_call_target="InvertDiagBlocksLowerTriangular" | custom-call | tf_op jit(solution)/shard_map/triangular_solve/custom-call.0 | solution.py:33
  195.9 2.9 %cholesky.111 = f32[32,32]{1,0:T(8,128)S(1)} custom-call(f32[32,32]{1,0:T(8,128)S(1)} %fusion.81), custom_call_target="Cholesky" | custom-call | tf_op jit(solution)/shard_map/jit(cholesky)/cholesky | solution.py:32
  200.1 2.4 %custom-call.11 = f32[1,32,32]{1,2,0:T(8,128)S(1)} custom-call(f32[1,32,32]{2,1,0:T(8,128)S(1)} %fusion.70), custom_call_target="InvertDiagBlocksLowerTriangular" | custom-call | tf_op jit(solution)/shard_map/triangular_solve/custom-call.0 | solution.py:33
  203.4 2.9 %cholesky.122 = f32[32,32]{1,0:T(8,128)S(1)} custom-call(f32[32,32]{1,0:T(8,128)S(1)} %fusion.78), custom_call_target="Cholesky" | custom-call | tf_op jit(solution)/shard_map/jit(cholesky)/cholesky | solution.py:32
  207.6 2.4 %custom-call.12 = f32[1,32,32]{1,2,0:T(8,128)S(1)} custom-call(f32[1,32,32]{2,1,0:T(8,128)S(1)} %fusion.71), custom_call_target="InvertDiagBlocksLowerTriangular" | custom-call | tf_op jit(solution)/shard_map/triangular_solve/custom-call.0 | solution.py:33
  210.8 2.9 %cholesky.133 = f32[32,32]{1,0:T(8,128)S(1)} custom-call(f32[32,32]{1,0:T(8,128)S(1)} %fusion.75), custom_call_target="Cholesky" | custom-call | tf_op jit(solution)/shard_map/jit(cholesky)/cholesky | solution.py:32
  219.2 14.0 %all_to_all.39 = f32[32,2,1248]{2,1,0:T(2,128)S(1)} all-to-all(f32[32,2,1248]{2,1,0:T(2,128)S(1)} %constant_dynamic-update-slice_fusion), channel_id=1, replica_groups=mesh['tm'=32,'slab'=4] {'tm'}, dimensions={0} | all-to-all | bytes 638976 | tf_op jit(solution)/shard_map/all_to_all | solution.py:81
  (118 shorter events, 40.1 us)
Async XLA Ops:
  33.0 4.3 %copy-start = (bf16[2,4,24,96,104]{4,3,2,1,0:T(8,128)(2,1)S(1)}, bf16[2,4,24,96,104]{4,3,2,1,0:T(8,128)(2,1)}, u32[]{:S(2)}) copy-start(bf16[2,4,24,96,104]{4,3,2,1,0:T(8,128)(2,1)} %squeeze.17) | copy-start | bytes 11501572
  37.3 5.1 %slice-start = ((s8[4718592]{0:T(1024)(128)(4,1)}), s8[4194304]{0:T(1024)(128)(4,1)S(1)}, s32[]{:S(2)}) async-start(s8[4718592]{0:T(1024)(128)(4,1)} %bitcast.289), calls=%async_computation.3 | async-start | bytes 8388608
  39.4 3.1 %slice-start.1 = ((s8[4718592]{0:T(1024)(128)(4,1)}), s8[524288]{0:T(1024)(128)(4,1)S(1)}, s32[]{:S(2)}) async-start(s8[4718592]{0:T(1024)(128)(4,1)} %bitcast.289), calls=%async_computation.4 | async-start | bytes 1048576
  59.4 16.1 %all-to-all-start = ((bf16[4,2,39936]{2,1,0:T(2,128)(2,1)}), bf16[4,2,39936]{2,1,0:T(2,128)(2,1)}, u32[]{:S(2)}, u32[]{:S(2)}) async-start(bf16[4,2,39936]{2,1,0:T(2,128)(2,1)} %reshape.57), calls=%async_computation | async-start | bytes 1277952 | tf_op jit(solution)/shard_map/all_to_all | solution.py:57
  88.3 6.6 %copy-start.1 = (bf16[2,4,96,8,26]{2,3,4,1,0:T(8,128)(2,1)S(1)}, bf16[2,4,96,8,26]{2,3,4,1,0:T(8,128)(2,1)}, u32[]{:S(2)}) copy-start(bf16[2,4,96,8,26]{2,3,4,1,0:T(8,128)(2,1)} %squeeze.18) | copy-start | bytes 958468
  88.3 6.6 %copy-start.2 = (f32[4,8,26,96]{3,2,1,0:T(8,128)S(1)}, f32[4,8,26,96]{3,2,1,0:T(8,128)}, u32[]{:S(2)}) copy-start(f32[4,8,26,96]{3,2,1,0:T(8,128)} %copy.35) | copy-start | bytes 958468
  98.3 19.0 %all-to-all-start.1 = ((f32[2,32,1248]{2,0,1:T(2,128)}), f32[2,32,1248]{2,0,1:T(2,128)S(1)}, u32[]{:S(2)}, u32[]{:S(2)}) async-start(f32[2,32,1248]{2,0,1:T(2,128)} %copy.47), calls=%async_computation.1 | async-start | bytes 655360 | tf_op jit(solution)/shard_map/all_to_all | solution.py:71
